TPU v7x, 512 devices: a whole 4x8x8 slice. The times are simulated.
512 devices in a mesh: expert: 128 (over z, y, core), tensor: 4 (over x).
Axes of the slice: x: 4, y: 8, z: 8, core: 2. Of those that a mesh axis runs over, the one named last changes fastest.
Arguments:
- tokens: bfloat16 [16384, 2880], P('expert', 'tensor'), may hold values from -6 to 6
- routes: int32 [16384, 4], P('expert'), may hold values from 0 to 127, all different within a row; in each aligned block of 128 rows (0 to 127, 128 to 255, ...) at most 5 rows name the same one
- route_gate_weight: int32 [16384, 4], P('expert'), may hold values from 1 to 65535
- up_frozen_matrix: bfloat16 [128, 2880, 1440], P('expert', None, 'tensor'), may hold values from -0.109375 to 0.109375
- down_frozen_matrix: bfloat16 [128, 1440, 2880], P('expert', 'tensor'), may hold values from -0.15625 to 0.15625
- up_adapter_input: bfloat16 [128, 2880, 64], P('expert', None, 'tensor'), may hold values from -0.109375 to 0.109375
- up_adapter_output: bfloat16 [128, 64, 1440], P('expert', None, 'tensor'), may hold values from -0.75 to 0.75
- down_adapter_input: bfloat16 [128, 1440, 64], P('expert', 'tensor'), may hold values from -0.15625 to 0.15625
- down_adapter_output: bfloat16 [128, 64, 2880], P('expert', None, 'tensor'), may hold values from -0.75 to 0.75
Outputs:
- mixed: bfloat16 [16384, 2880], P('expert', 'tensor')
Inputs may be any that keep to these rules, and one draw needn't show every extreme that they name: `routes`: each row names 4 different experts; among the 128 rows of one block no expert is named more than 5 times, a bound that some expert reaches in some of these blocks.
All inputs are finite; a program needn't handle non-finite values.
Results may differ from a plain program's by a relative error of at most 0.018.
Values may be sent and summed in bfloat16 or wider, within the bound.
A program may use at most 64 MiB of HBM per device.

v0:
```python
import jax
import jax.numpy as jnp
from jax import lax
from jax.sharding import PartitionSpec as P


def local(
    tokens,
    routes,
    route_gate_weight,
    up_frozen_matrix,
    down_frozen_matrix,
    up_adapter_input,
    up_adapter_output,
    down_adapter_input,
    down_adapter_output,
):
    tok_rows, quarter = tokens.shape
    fanout = routes.shape[1]
    experts_total = up_frozen_matrix.shape[0] * lax.axis_size("expert")
    capacity = 5 * fanout * tok_rows // (4 * experts_total)
    expert_ids = routes.reshape(-1)
    one_hot = (expert_ids[:, None] == jnp.arange(experts_total, dtype=jnp.int32)[None, :]).astype(
        jnp.int32
    )
    earlier = jnp.cumsum(one_hot, axis=0) - one_hot
    position = jnp.sum(earlier * one_hot, axis=1)
    target = expert_ids * capacity + position
    source_row = jnp.arange(tok_rows * fanout, dtype=jnp.int32) // fanout
    slot_token = (
        jnp.full((experts_total * capacity,), tok_rows, jnp.int32).at[target].set(source_row)
    )
    width = quarter * lax.axis_size("tensor")
    whole = lax.all_gather(tokens, "tensor", axis=1, tiled=True)
    padded = jnp.concatenate([whole, jnp.zeros((1, width), jnp.bfloat16)], axis=0)
    outgoing = jnp.take(padded, slot_token, axis=0).reshape(experts_total, capacity, width)
    received_rows = lax.all_to_all(
        outgoing, "expert", split_axis=0, concat_axis=0, tiled=True
    ).reshape(-1, width)
    up_projected = jnp.dot(received_rows, up_frozen_matrix[0], preferred_element_type=jnp.float32)
    adapter_codes = jnp.dot(
        received_rows, up_adapter_input[0], preferred_element_type=jnp.float32
    ).astype(jnp.bfloat16)
    every_adapter_code = lax.all_gather(adapter_codes, "tensor", axis=1, tiled=True)
    up_projected = up_projected + 0.5 * jnp.dot(
        every_adapter_code, up_adapter_output[0], preferred_element_type=jnp.float32
    )
    hidden_state = (up_projected * jax.nn.sigmoid(1.702 * up_projected)).astype(jnp.bfloat16)
    adapter_terms = jnp.dot(hidden_state, down_adapter_input[0], preferred_element_type=jnp.float32)
    down_adapter_codes = lax.psum(adapter_terms.astype(jnp.bfloat16), "tensor")
    partial_value = jnp.dot(hidden_state, down_frozen_matrix[0], preferred_element_type=jnp.float32)
    summed_output = lax.psum_scatter(
        partial_value.astype(jnp.bfloat16), "tensor", scatter_dimension=1, tiled=True
    ).astype(jnp.float32)
    expert_out = (
        summed_output
        + 0.5
        * jnp.dot(down_adapter_codes, down_adapter_output[0], preferred_element_type=jnp.float32)
    ).astype(jnp.bfloat16)
    returned = lax.all_to_all(
        expert_out.reshape(experts_total, capacity, quarter),
        "expert",
        split_axis=0,
        concat_axis=0,
        tiled=True,
    )
    returned = returned.reshape(-1, quarter)
    scale = route_gate_weight.astype(jnp.float32) / 65536.0
    picked = (
        jnp.take(returned, target, axis=0).astype(jnp.float32).reshape(tok_rows, fanout, quarter)
    )
    mixed = jnp.sum(picked * scale[:, :, None], axis=1)
    return mixed.astype(jnp.bfloat16)


def solution(mesh):
    return jax.shard_map(
        local,
        mesh=mesh,
        in_specs=(
            P("expert", "tensor"),
            P("expert", None),
            P("expert", None),
            P("expert", None, "tensor"),
            P("expert", "tensor", None),
            P("expert", None, "tensor"),
            P("expert", None, "tensor"),
            P("expert", "tensor", None),
            P("expert", None, "tensor"),
        ),
        out_specs=P("expert", "tensor"),
        check_vma=False,
    )
```

profile of v0, /device:TPU:1, one launch (start us, length us, event | category | flops | bytes accessed | tf_op | source)
XLA Modules:
  0.0 408.6 jit_solution(3181158299192170875)
XLA Ops:
  9.3 2.4 scatter_custom_fusion
  11.8 11.7 %all_gather.6 = bf16[128,2880]{0,1:T(8,128)(2,1)S(1)} all-gather(bf16[128,720]{0,1:T(8,128)(2,1)} %param.9), channel_id=1, replica_groups=mesh['expert'=128,'tensor'=4] {'tensor'}, dimensions={1}, use_global_device_ids=true | all-gather | bytes 921600 | tf_op jit(solution)/shard_map/all_gather | solution.py:34
  23.5 1.2 copy.38
  24.7 1.2 concatenate.3
  25.9 4.6 %gather_fusion = bf16[640,2880]{1,0:T(8,128)(2,1)} fusion(bf16[129,2880]{1,0:T(8,128)(2,1)S(1)} %concatenate.3, s32[1024]{0:T(1024)S(1)} %pad_clamp_fusion.1), kind=kCustom, calls=%fused_computation | custom fusion | bytes 7375360 | tf_op jit(solution)/shard_map/jit(_take)/gather | solution.py:36
  30.5 7.4 %gather.13 = bf16[128,5,2880]{2,1,0:T(8,128)(2,1)} reshape(bf16[640,2880]{1,0:T(8,128)(2,1)} %gather_fusion) | data formatting | bytes 7372800 | tf_op jit(solution)/shard_map/jit(_take)/gather | solution.py:36
  38.1 3.5 broadcast_select_fusion
  41.6 156.7 %all_to_all.10 = bf16[128,5,2880]{2,1,0:T(8,128)(2,1)} all-to-all(bf16[128,5,2880]{2,1,0:T(8,128)(2,1)S(1)} %broadcast_select_fusion), channel_id=1, replica_groups=mesh['expert'=128,'tensor'=4] {'expert'}, dimensions={0} | all-to-all | bytes 7372800 | tf_op jit(solution)/shard_map/all_to_all | solution.py:37
  198.3 8.0 %reshape.86 = bf16[640,2880]{1,0:T(8,128)(2,1)} reshape(bf16[128,5,2880]{2,1,0:T(8,128)(2,1)} %all_to_all.10) | data formatting | bytes 7372800 | tf_op jit(solution)/shard_map/reshape | solution.py:39
  206.2 4.8 %fusion.1 = f32[640,360]{0,1:T(8,128)S(1)} fusion(bf16[640,2880]{1,0:T(8,128)(2,1)} %reshape.86, bf16[1,2880,360]{1,2,0:T(8,128)(2,1)} %param.12), kind=kOutput, calls=%fused_computation.6 | convolution fusion | flops 1327104000 | bytes 6681600 | tf_op jit(solution)/shard_map/dot_general | solution.py:40
  211.1 1.1 convolution_convert_fusion.2
  212.2 9.3 %all_gather.7 = bf16[640,64]{0,1:T(8,128)(2,1)S(1)} all-gather(bf16[640,16]{0,1:T(8,128)(2,1)S(1)} %convolution_convert_fusion.2), channel_id=1, replica_groups=mesh['expert'=128,'tensor'=4] {'tensor'}, dimensions={1}, use_global_device_ids=true | all-gather | bytes 102400 | tf_op jit(solution)/shard_map/all_gather | solution.py:44
  223.0 4.1 %convolution_convert_fusion = bf16[640,2880]{0,1:T(8,128)(2,1)} fusion(bf16[640,360]{0,1:T(8,128)(2,1)S(1)} %multiply_convert_fusion, bf16[1,360,2880]{2,1,0:T(8,128)(2,1)S(1)} %copy-done), kind=kOutput, calls=%fused_computation.4 | convolution fusion | flops 1328947200 | bytes 6220800 | tf_op jit(solution)/shard_map/dot_general | solution.py:51
  227.2 50.8 %all-reduce.3.cloned.1.call-done = bf16[640,64]{0,1:T(8,128)(2,1)} async-done(((bf16[640,64]{0,1:T(8,128)(2,1)}), bf16[640,64]{0,1:T(8,128)(2,1)}) %all-reduce.3.cloned.1.call-update) | async-done | bytes 81936 | tf_op jit(solution)/shard_map/psum | solution.py:50
  277.9 53.7 %reduce-scatter.2.cloned.1.call-done = bf16[640,720]{0,1:T(8,128)(2,1)} async-done(((bf16[640,2880]{0,1:T(8,128)(2,1)}), bf16[640,720]{0,1:T(8,128)(2,1)}) %reduce-scatter.2.cloned.1.call-update) | async-done | bytes 921616 | tf_op jit(solution)/shard_map/reduce_scatter | solution.py:52
  331.6 2.6 add_convert_fusion
  334.3 1.6 copy.39
  335.9 1.4 reshape.87
  337.2 14.6 %all-to-all-start.1 = ((bf16[128,5,720]{2,1,0:T(8,128)(2,1)}), bf16[128,5,720]{2,1,0:T(8,128)(2,1)}, u32[]{:S(2)}, u32[]{:S(2)}) async-start(bf16[128,5,720]{2,1,0:T(8,128)(2,1)} %reshape.87), calls=%async_computation.2 | async-start | bytes 3145728 | tf_op jit(solution)/shard_map/all_to_all | solution.py:60
  352.4 40.4 %all-to-all-done.1 = bf16[128,5,720]{2,1,0:T(8,128)(2,1)} async-done(((bf16[128,5,720]{2,1,0:T(8,128)(2,1)}), bf16[128,5,720]{2,1,0:T(8,128)(2,1)}, u32[]{:S(2)}, u32[]{:S(2)}) %all-to-all-start.1) | async-done | bytes 921632 | tf_op jit(solution)/shard_map/all_to_all | solution.py:60
  392.8 2.4 reshape.88
  395.3 2.7 gather_fusion.1
  398.0 1.7 gather.15
  399.7 1.3 multiply_reduce_fusion
  (51 shorter events, 5.8 us)
Async XLA Ops:
  6.5 216.5 %copy-start = (bf16[1,360,2880]{2,1,0:T(8,128)(2,1)S(1)}, bf16[1,360,2880]{2,1,0:T(8,128)(2,1)}, u32[]{:S(2)}) copy-start(bf16[1,360,2880]{2,1,0:T(8,128)(2,1)} %param.13) | copy-start | bytes 6220804
  6.5 271.4 %all-reduce.3.cloned.1.call-start = ((), (), s32[]{:S(2)}) async-start(), calls=%async_computation.4 | async-start | bytes 163840 | tf_op jit(solution)/shard_map/psum | solution.py:50
  206.2 4.8 %copy-start.1 = (bf16[640,2880]{1,0:T(8,128)(2,1)S(1)}, bf16[640,2880]{1,0:T(8,128)(2,1)}, u32[]{:S(2)}) copy-start(bf16[640,2880]{1,0:T(8,128)(2,1)} %reshape.86) | copy-start | bytes 11059204
  206.2 4.8 %copy-start.3 = (bf16[1,2880,16]{1,2,0:T(8,128)(2,1)S(1)}, bf16[1,2880,16]{1,2,0:T(8,128)(2,1)}, u32[]{:S(2)}) copy-start(bf16[1,2880,16]{1,2,0:T(8,128)(2,1)} %param.14) | copy-start | bytes 276484
  211.1 10.3 %copy-start.7 = (bf16[1,64,360]{2,1,0:T(8,128)(2,1)S(1)}, bf16[1,64,360]{2,1,0:T(8,128)(2,1)}, u32[]{:S(2)}) copy-start(bf16[1,64,360]{2,1,0:T(8,128)(2,1)} %param.15) | copy-start | bytes 138244
  211.1 10.8 %copy-start.4 = (bf16[1,360,64]{1,2,0:T(8,128)(2,1)S(1)}, bf16[1,360,64]{1,2,0:T(8,128)(2,1)}, u32[]{:S(2)}) copy-start(bf16[1,360,64]{1,2,0:T(8,128)(2,1)} %param.16) | copy-start | bytes 138244
  222.8 108.8 %reduce-scatter.2.cloned.1.call-start = ((), (), s32[]{:S(2)}) async-start(), calls=%async_computation.3 | async-start | bytes 4608000 | tf_op jit(solution)/shard_map/reduce_scatter | solution.py:52
  227.1 104.5 %copy-start.2 = (bf16[1,64,720]{2,1,0:T(8,128)(2,1)S(1)}, bf16[1,64,720]{2,1,0:T(8,128)(2,1)}, u32[]{:S(2)}) copy-start(bf16[1,64,720]{2,1,0:T(8,128)(2,1)} %param.17) | copy-start | bytes 276484
  334.2 17.8 %copy-start.5 = (s32[128,4]{0,1:T(4,128)S(1)}, s32[128,4]{0,1:T(4,128)}, u32[]{:S(2)}) copy-start(s32[128,4]{0,1:T(4,128)} %param.10) | copy-start | bytes 6148
  334.2 18.0 %copy-start.6 = (s32[128,4]{0,1:T(4,128)S(1)}, s32[128,4]{0,1:T(4,128)}, u32[]{:S(2)}) copy-start(s32[128,4]{0,1:T(4,128)} %param.11) | copy-start | bytes 6148
  337.2 55.6 %all-to-all-start.1 = ((bf16[128,5,720]{2,1,0:T(8,128)(2,1)}), bf16[128,5,720]{2,1,0:T(8,128)(2,1)}, u32[]{:S(2)}, u32[]{:S(2)}) async-start(bf16[128,5,720]{2,1,0:T(8,128)(2,1)} %reshape.87), calls=%async_computation.2 | async-start | bytes 3145728 | tf_op jit(solution)/shard_map/all_to_all | solution.py:60
Sparse Core Ops, SparseCore 0:
  222.9 55.0 all-reduce.2
  281.0 50.5 reduce-scatter.1
where the time goes:
time: 410 us; the launch traced here: 409 us
  blocking collectives  178 us (43%)
  waiting for transfers between devices  145 us (35%)
  local copies, waits for them, and re-layouts  37.6 us (9%)
  starting transfers between devices  14.9 us (4%)
  matrix products  13.9 us (3%)
  between operations  13.6 us (3%)
  other arithmetic  6.02 us (1%)
    all_to_all x1, blocking collectives, local(): lax.all_to_all(outgoing, 'expert', split_axis=0, concat_axis=0, tiled=True)  157 us
    reduce_scatter x1, waiting for transfers between devices, local(): lax.psum_scatter(partial_value.astype(jnp.bfloat16), 'tensor', scatter_di...  53.7 us
    psum x1, waiting for transfers between devices, local(): down_adapter_codes = lax.psum(adapter_terms.astype(jnp.bfloat16), 'tensor')  50.8 us
    all_to_all x1, waiting for transfers between devices, local(): lax.all_to_all(expert_out.reshape(experts_total, capacity, quarter), 'exp...  40.4 us
    all_to_all x1, starting transfers between devices, local(): lax.all_to_all(expert_out.reshape(experts_total, capacity, quarter), 'exp...  14.6 us
    gather x2, local copies, waits for them, and re-layouts, local(): jnp.take(padded, slot_token, axis=0).reshape(experts_total, capacity, width)  12 us
    all_gather x1, blocking collectives, local(): whole = lax.all_gather(tokens, 'tensor', axis=1, tiled=True)  11.7 us
    all_gather x1, blocking collectives, local(): lax.all_gather(adapter_codes, 'tensor', axis=1, tiled=True)  9.25 us
  transfers between devices with their start and end apart: 3, of which 3 were waited for; matrix products, arithmetic and copies ran while one was open for 1% of the time, Pallas kernels for 0%

commit v1 on v0

v1 whole, which is shorter than its diff:
```python
import functools

import jax
import jax.numpy as jnp
from jax import lax
from jax.experimental import pallas as pl
from jax.experimental.pallas import tpu as pltpu
from jax.sharding import PartitionSpec as P

NZ, NY, NX = 8, 8, 4
CAP = 5
SLOTS = 2 * CAP
LANES = 128
BF16, F32, I32 = jnp.bfloat16, jnp.float32, jnp.int32

NN = (((1,), (0,)), ((), ()))
NT = (((1,), (1,)), ((), ()))
TN = (((0,), (0,)), ((), ()))

(OUT_Y, OUT_Z, OUT_RIGHT, OUT_LEFT, OUT_RIGHT2, OUT_LEFT2, SUM_RIGHT, SUM_LEFT, SUM_RIGHT2, SUM_LEFT2,
 BACK_Z, BACK_Y, MERGE) = range(13)
TOK, META, UP_IN, DOWN_OUT = range(4)


def dot(a, b, dims):
    return lax.dot_general(a, b, dims, preferred_element_type=F32)


def kernel(chunks, routes_ref, gates_ref, tok_ref, wup_hbm, wdn_hbm, aup_ref, bup_ref, adn_ref, bdn_ref, out_ref,
           tok2, meta, sel, ghi, glo, perm, wraw, wdraw, afull, bfull, w1, w2,
           ysend, yrecv, zsend, gath, acc, hid, part, half_l, half_r, full_l, full_r,
           esend, zback, yback, rback, msend, mrecv, own,
           send_sem, recv_sem, send_once, recv_once, local_sem):
    expert, x = lax.axis_index("expert"), lax.axis_index("tensor")
    z, y, core = expert // (2 * NY), (expert // 2) % NY, expert % 2
    right, left, across = (x + 1) % NX, (x + NX - 1) % NX, (x + 2) % NX
    quarter, tokens = tok_ref.shape
    hidden = bup_ref.shape[1]
    rank = bup_ref.shape[0]
    part_rank = aup_ref.shape[0]
    code_at = w1.shape[1] - rank
    ygroup, zgroup = SLOTS * NZ, SLOTS * NY
    rows = ygroup * NY
    half = rows // 2
    last = quarter - (chunks - 1) * LANES

    def at(zz, yy, cc):
        return {"expert": (zz * NY + yy) * 2 + cc}

    sibling = at(z, y, 1 - core)

    def send(src, dst, kind, k, device):
        pltpu.make_async_remote_copy(
            src_ref=src, dst_ref=dst, send_sem=send_sem.at[kind, k], recv_sem=recv_sem.at[kind, k],
            device_id=device, device_id_type=pl.DeviceIdType.MESH).start()

    def arrived(ref, kind, k):
        pltpu.make_async_copy(ref, ref, recv_sem.at[kind, k]).wait()

    def sent(ref, kind, k):
        pltpu.make_async_copy(ref, ref, send_sem.at[kind, k]).wait()

    def send_one(src, dst, which, device):
        pltpu.make_async_remote_copy(
            src_ref=src, dst_ref=dst, send_sem=send_once.at[which], recv_sem=recv_once.at[which],
            device_id=device, device_id_type=pl.DeviceIdType.MESH).start()

    load_up = pltpu.make_async_copy(wup_hbm, wraw, local_sem.at[0])
    load_down = pltpu.make_async_copy(wdn_hbm, wdraw, local_sem.at[1])
    load_up.start()
    load_down.start()

    barrier = pltpu.get_barrier_semaphore()

    def greet(device):
        pl.semaphore_signal(barrier, inc=1, device_id=device, device_id_type=pl.DeviceIdType.MESH)

    greet(sibling)

    @pl.loop(1, NY)
    def _(j):
        greet(at(z, (y + j) % NY, core))

    @pl.loop(1, NZ)
    def _(j):
        greet(at((z + j) % NZ, y, core))

    @pl.loop(1, NX)
    def _(j):
        greet({"tensor": (x + j) % NX})

    meta[0, 0:4, :] = routes_ref[...]
    meta[0, 4:8, :] = gates_ref[...]
    tok2[0:quarter, 0:tokens] = tok_ref[...]
    tok2[quarter:, :] = jnp.zeros_like(tok2[quarter:, :])
    afull[pl.ds(pl.multiple_of(x * part_rank, part_rank), part_rank), :] = aup_ref[...]
    bfull[x] = bdn_ref[...]

    pl.semaphore_wait(barrier, NY + NZ + NX - 2)

    send_one(meta.at[0], meta.at[1], META, sibling)
    send_one(tok_ref, tok2.at[0:quarter, tokens:2 * tokens], TOK, sibling)

    @pl.loop(1, NX)
    def _(j):
        mine = pl.ds(pl.multiple_of(x * part_rank, part_rank), part_rank)
        send_one(aup_ref, afull.at[mine], UP_IN, {"tensor": (x + j) % NX})
        send_one(bdn_ref, bfull.at[x], DOWN_OUT, {"tensor": (x + j) % NX})

    row = lax.broadcasted_iota(I32, (ygroup, rows), 0)
    column = lax.broadcasted_iota(I32, (ygroup, rows), 1)
    for a in range(NY):
        source = (row % NZ) * ygroup + (row // NZ) * NZ + a
        perm[a * ygroup:(a + 1) * ygroup, :] = (column == source).astype(F32).astype(BF16)

    pltpu.make_async_copy(meta.at[0], meta.at[1], recv_once.at[META]).wait()

    before = (lax.broadcasted_iota(I32, (tokens, tokens), 0)
              < lax.broadcasted_iota(I32, (tokens, tokens), 1)).astype(F32).astype(BF16)
    slot_row = lax.broadcasted_iota(I32, (CAP * NZ, tokens), 0)
    for yy in range(NY):
        expert_id = ((slot_row % NZ) * NY + yy) * 2 + core
        picks, gates = [], []
        for src in range(2):
            hit = jnp.zeros((CAP * NZ, tokens), I32)
            gate = jnp.zeros((CAP * NZ, tokens), I32)
            for k in range(4):
                same = meta[src, k:k + 1, :] == expert_id
                hit = jnp.where(same, 1, hit)
                gate = jnp.where(same, meta[src, 4 + k:5 + k, :], gate)
            position = dot(hit.astype(F32).astype(BF16), before, NN)
            pick = jnp.where(position == (slot_row // NZ).astype(F32), hit, 0)
            picks.append(pick)
            gates.append(gate * pick)
        none = jnp.zeros((CAP * NZ, tokens), I32)

        def both(values):
            grid = jnp.concatenate([jnp.concatenate([values[0], none], axis=1),
                                    jnp.concatenate([none, values[1]], axis=1)], axis=0)
            return grid.astype(F32)

        block = slice(yy * ygroup, (yy + 1) * ygroup)
        sel[block, :] = both(picks).astype(BF16)
        ghi[block, :] = (both([g >> 8 for g in gates]) * (1.0 / 256.0)).astype(BF16)
        glo[block, :] = (both([g & 255 for g in gates]) * (1.0 / 65536.0)).astype(BF16)

    pltpu.make_async_copy(tok_ref, tok2.at[0:quarter, tokens:2 * tokens], recv_once.at[TOK]).wait()

    def yblock(j):
        return pl.ds(pl.multiple_of(j * ygroup, 16), ygroup)

    def zblock(j):
        return pl.ds(pl.multiple_of(j * zgroup, 16), zgroup)

    def choose(k):
        feats = pl.ds(pl.multiple_of(k * LANES, LANES), LANES)
        ysend[k] = dot(sel[...], tok2[feats, :], NT).astype(BF16)

        @pl.loop(1, NY)
        def _(j):
            yy = (y + j) % NY
            send(ysend.at[k, yblock(yy)], yrecv.at[k, yblock(y)], OUT_Y, k, at(z, yy, core))

        yrecv[k, yblock(y), :] = ysend[k, yblock(y), :]

    def pass_z(k):
        arrived(yrecv.at[k, 0:rows - ygroup], OUT_Y, k)
        zsend[k] = dot(perm[...], yrecv[k], NN).astype(BF16)

        @pl.loop(1, NZ)
        def _(j):
            zz = (z + j) % NZ
            send(zsend.at[k, zblock(zz)], gath.at[k, x, zblock(z)], OUT_Z, k, at(zz, y, core))

        gath[k, x, zblock(z), :] = zsend[k, zblock(z), :]

    def spread(k):
        arrived(gath.at[k, x, 0:rows - zgroup], OUT_Z, k)
        send(gath.at[k, x], gath.at[k, x], OUT_RIGHT, k, {"tensor": right})
        send(gath.at[k, x], gath.at[k, x], OUT_LEFT, k, {"tensor": left})

    def forward(k):
        arrived(gath.at[k, left], OUT_RIGHT, k)
        send(gath.at[k, left, 0:half], gath.at[k, left, 0:half], OUT_RIGHT2, k, {"tensor": right})
        arrived(gath.at[k, right], OUT_LEFT, k)
        send(gath.at[k, right, half:rows], gath.at[k, right, half:rows], OUT_LEFT2, k, {"tensor": left})

    def multiply(k):
        arrived(gath.at[k, across, 0:half], OUT_RIGHT2, k)
        arrived(gath.at[k, across, half:rows], OUT_LEFT2, k)
        lhs = jnp.concatenate([gath[k, q] for q in range(NX)], axis=1)
        acc[...] += dot(lhs, w1[k], NT)

    def arrange(raw, weights):
        for k in range(chunks):
            width = min(LANES, quarter - k * LANES)
            for q in range(NX):
                first = q * quarter + k * LANES
                weights[k, 0:hidden, q * LANES:q * LANES + width] = raw[0, :, first:first + width]

    def arrange_up():
        load_up.wait()
        w1[...] = jnp.zeros_like(w1)
        arrange(wraw, w1)
        pltpu.make_async_copy(afull.at[0:(NX - 1) * part_rank], afull.at[0:(NX - 1) * part_rank],
                              recv_once.at[UP_IN]).wait()
        for k in range(chunks):
            width = min(LANES, quarter - k * LANES)
            for q in range(NX):
                first = q * quarter + k * LANES
                w1[k, code_at:, q * LANES:q * LANES + width] = afull[:, first:first + width]

    def arrange_down():
        load_down.wait()
        w2[...] = jnp.zeros_like(w2)
        arrange(wdraw, w2)
        pltpu.make_async_copy(bfull.at[0:NX - 1], bfull.at[0:NX - 1], recv_once.at[DOWN_OUT]).wait()
        for k in range(chunks):
            width = min(LANES, quarter - k * LANES)
            for q in range(NX):
                w2[k, code_at:, q * LANES:q * LANES + width] = bfull[q, :, k * LANES:k * LANES + width]

    choose(0)
    choose(1)
    acc[...] = jnp.zeros_like(acc)
    hid[...] = jnp.zeros_like(hid)
    arrange_up()

    def step(tick, stage, delay):
        k = tick - delay

        @pl.when((k >= 0) & (k < chunks))
        def _():
            stage(k)

    @pl.loop(0, chunks + 3)
    def _(t):
        step(t, spread, 1)
        step(t, pass_z, 0)
        step(t, choose, -2)

        @pl.when(t == 0)
        def _():
            arrange_down()

        step(t, forward, 2)
        step(t, multiply, 3)

    codes = acc[:, code_at:].astype(BF16)
    upward = acc[:, 0:hidden] + 0.5 * dot(codes, bup_ref[...], NN)
    units = (upward * jax.nn.sigmoid(1.702 * upward)).astype(BF16)
    hid[:, 0:hidden] = units
    hid[:, code_at:] = (0.5 * dot(units, adn_ref[...], NT)).astype(BF16)

    def partial(k):
        product = dot(hid[...], w2[k], NN).astype(BF16)
        for q in range(NX):
            part[k, q] = product[:, q * LANES:(q + 1) * LANES]
        send(part.at[k, across, 0:half], half_l.at[k], SUM_RIGHT, k, {"tensor": right})
        send(part.at[k, across, half:rows], half_r.at[k], SUM_LEFT, k, {"tensor": left})

    def add_half(k):
        arrived(half_l.at[k], SUM_RIGHT, k)
        part[k, right, 0:half, :] = (part[k, right, 0:half, :].astype(F32) + half_l[k].astype(F32)).astype(BF16)
        send(part.at[k, right], full_l.at[k], SUM_RIGHT2, k, {"tensor": right})
        arrived(half_r.at[k], SUM_LEFT, k)
        part[k, left, half:rows, :] = (part[k, left, half:rows, :].astype(F32) + half_r[k].astype(F32)).astype(BF16)
        send(part.at[k, left], full_r.at[k], SUM_LEFT2, k, {"tensor": left})

    def add_full(k):
        arrived(full_l.at[k], SUM_RIGHT2, k)
        arrived(full_r.at[k], SUM_LEFT2, k)
        total = part[k, x].astype(F32) + full_l[k].astype(F32) + full_r[k].astype(F32)
        esend[k] = total.astype(BF16)

        @pl.loop(1, NZ)
        def _(j):
            zz = (z + j) % NZ
            send(esend.at[k, zblock(zz)], zback.at[k, zblock(z)], BACK_Z, k, at(zz, y, core))

        zback[k, zblock(z), :] = esend[k, zblock(z), :]

    def pass_y(k):
        arrived(zback.at[k, 0:rows - zgroup], BACK_Z, k)
        yback[k] = dot(perm[...], zback[k], NN).astype(BF16)

        @pl.loop(1, NY)
        def _(j):
            yy = (y + j) % NY
            send(yback.at[k, yblock(yy)], rback.at[k, yblock(y)], BACK_Y, k, at(z, yy, core))

        rback[k, yblock(y), :] = yback[k, yblock(y), :]

    def mix(k):
        arrived(rback.at[k, 0:rows - ygroup], BACK_Y, k)
        mixed = dot(rback[k], ghi[...], TN) + dot(rback[k], glo[...], TN)
        own[k] = mixed[:, 0:tokens]
        msend[k] = mixed[:, tokens:]
        send(msend.at[k], mrecv.at[k], MERGE, k, sibling)

    @pl.loop(0, chunks + 4)
    def _(t):
        step(t, add_full, 2)
        step(t, partial, 0)
        step(t, add_half, 1)
        step(t, pass_y, 3)
        step(t, mix, 4)

    for k in range(chunks):
        width = min(LANES, quarter - k * LANES)
        arrived(mrecv.at[k], MERGE, k)
        out_ref[k * LANES:k * LANES + width, :] = (own[k, 0:width, :] + mrecv[k, 0:width, :]).astype(BF16)

    @pl.loop(0, chunks)
    def _(k):
        sent(ysend.at[k, 0:rows - ygroup], OUT_Y, k)
        sent(zsend.at[k, 0:rows - zgroup], OUT_Z, k)
        sent(gath.at[k, 0], OUT_RIGHT, k)
        sent(gath.at[k, 0], OUT_LEFT, k)
        sent(gath.at[k, 0, 0:half], OUT_RIGHT2, k)
        sent(gath.at[k, 0, 0:half], OUT_LEFT2, k)
        sent(half_l.at[k], SUM_RIGHT, k)
        sent(half_r.at[k], SUM_LEFT, k)
        sent(full_l.at[k], SUM_RIGHT2, k)
        sent(full_r.at[k], SUM_LEFT2, k)
        sent(esend.at[k, 0:rows - zgroup], BACK_Z, k)
        sent(yback.at[k, 0:rows - ygroup], BACK_Y, k)
        sent(msend.at[k], MERGE, k)

    pltpu.make_async_copy(meta.at[0], meta.at[1], send_once.at[META]).wait()
    pltpu.make_async_copy(tok_ref, tok2.at[0:quarter, tokens:2 * tokens], send_once.at[TOK]).wait()
    pltpu.make_async_copy(afull.at[0:(NX - 1) * part_rank], afull.at[0:(NX - 1) * part_rank],
                          send_once.at[UP_IN]).wait()
    pltpu.make_async_copy(bfull.at[0:NX - 1], bfull.at[0:NX - 1], send_once.at[DOWN_OUT]).wait()


def local(tokens, routes, gates, wup, wdn, aup, bup, adn, bdn):
    count, quarter = tokens.shape
    hidden, rank = wup.shape[2], bup.shape[1]
    part_rank = aup.shape[2]
    chunks = -(-quarter // LANES)
    rows = SLOTS * NY * NZ
    inner = -(-hidden // LANES) * LANES + rank
    grid = (chunks, rows, LANES)
    vmem, hbm = pl.BlockSpec(memory_space=pltpu.VMEM), pl.BlockSpec(memory_space=pl.ANY)
    out = pl.pallas_call(
        functools.partial(kernel, chunks),
        out_shape=jax.ShapeDtypeStruct((quarter, count), BF16),
        in_specs=[vmem, vmem, vmem, hbm, hbm, vmem, vmem, vmem, vmem],
        out_specs=vmem,
        scratch_shapes=[
            pltpu.VMEM((chunks * LANES, 2 * count), BF16),
            pltpu.VMEM((2, 8, count), I32),
            pltpu.VMEM((rows, 2 * count), BF16),
            pltpu.VMEM((rows, 2 * count), BF16),
            pltpu.VMEM((rows, 2 * count), BF16),
            pltpu.VMEM((rows, rows), BF16),
            pltpu.VMEM((1, hidden, NX * quarter), BF16),
            pltpu.VMEM((1, hidden, NX * quarter), BF16),
            pltpu.VMEM((rank, NX * quarter), BF16),
            pltpu.VMEM((NX, rank, quarter), BF16),
            pltpu.VMEM((chunks, inner, NX * LANES), BF16),
            pltpu.VMEM((chunks, inner, NX * LANES), BF16),
            pltpu.VMEM(grid, BF16),
            pltpu.VMEM(grid, BF16),
            pltpu.VMEM(grid, BF16),
            pltpu.VMEM((chunks, NX, rows, LANES), BF16),
            pltpu.VMEM((rows, inner), F32),
            pltpu.VMEM((rows, inner), BF16),
            pltpu.VMEM((chunks, NX, rows, LANES), BF16),
            pltpu.VMEM((chunks, rows // 2, LANES), BF16),
            pltpu.VMEM((chunks, rows // 2, LANES), BF16),
            pltpu.VMEM(grid, BF16),
            pltpu.VMEM(grid, BF16),
            pltpu.VMEM(grid, BF16),
            pltpu.VMEM(grid, BF16),
            pltpu.VMEM(grid, BF16),
            pltpu.VMEM(grid, BF16),
            pltpu.VMEM((chunks, LANES, count), F32),
            pltpu.VMEM((chunks, LANES, count), F32),
            pltpu.VMEM((chunks, LANES, count), F32),
            pltpu.SemaphoreType.DMA((13, chunks)),
            pltpu.SemaphoreType.DMA((13, chunks)),
            pltpu.SemaphoreType.DMA((4,)),
            pltpu.SemaphoreType.DMA((4,)),
            pltpu.SemaphoreType.DMA((2,)),
        ],
        compiler_params=pltpu.CompilerParams(
            collective_id=0, has_side_effects=True, vmem_limit_bytes=50 * 1024 * 1024),
        cost_estimate=pl.CostEstimate(flops=8 * 10**9, bytes_accessed=6 * 10**6, transcendentals=0),
    )(routes.T, gates.T, tokens.T, jnp.swapaxes(wup, 1, 2), wdn, aup[0].T, bup[0], adn[0].T, bdn[0])
    return out.T


def solution(mesh):
    return jax.shard_map(
        local,
        mesh=mesh,
        in_specs=(
            P("expert", "tensor"),
            P("expert", None),
            P("expert", None),
            P("expert", None, "tensor"),
            P("expert", "tensor", None),
            P("expert", None, "tensor"),
            P("expert", None, "tensor"),
            P("expert", "tensor", None),
            P("expert", None, "tensor"),
        ),
        out_specs=P("expert", "tensor"),
        check_vma=False,
    )
```

time: 410 us -> 147 us (0.36)
  blocking collectives: 178 us -> 0 us
  waiting for transfers between devices: 145 us -> 0 us
  Pallas kernels: 0 us -> 139 us
  local copies, waits for them, and re-layouts: 37.6 us -> 7.94 us
  starting transfers between devices: 14.9 us -> 0 us
  matrix products: 13.9 us -> 0 us
  between operations: 13.6 us -> 0.02 us
  other arithmetic: 6.02 us -> 0 us
    all_to_all x1 -> x0, blocking collectives: 157 us -> none  [local(): lax.all_to_all(outgoing, 'expert', split_axis=0, concat_axis=0, tiled=True)]
    pallas_call x0 -> x1, Pallas kernels: none -> 139 us  [local(): pl.pallas_call(functools.partial(kernel, chunks), out_shape=jax.ShapeDtyp...]
    reduce_scatter x1 -> x0, waiting for transfers between devices: 53.7 us -> none  [local(): lax.psum_scatter(partial_value.astype(jnp.bfloat16), 'tensor', scatter_di...]
    psum x1 -> x0, waiting for transfers between devices: 50.8 us -> none  [local(): down_adapter_codes = lax.psum(adapter_terms.astype(jnp.bfloat16), 'tensor')]
    all_to_all x1 -> x0, waiting for transfers between devices: 40.4 us -> none  [local(): lax.all_to_all(expert_out.reshape(experts_total, capacity, quarter), 'exp...]
    all_gather x2 -> x0, blocking collectives: 21 us -> none  [the longest x1 11.7 us: local(): whole = lax.all_gather(tokens, 'tensor', axis=1, tiled=True)]
    gather x4 -> x0, local copies, waits for them, and re-layouts: 16.4 us -> none  [the longest x2 12 us: local(): jnp.take(padded, slot_token, axis=0).reshape(experts_total, capacity, width)]
    all_to_all x1 -> x0, starting transfers between devices: 14.6 us -> none  [local(): lax.all_to_all(expert_out.reshape(experts_total, capacity, quarter), 'exp...]
  transfers between devices with their start and end apart: 3 -> 0, of which waited for: 3 -> 0; matrix products, arithmetic and copies ran while one was open for 1% -> 0% of each run, Pallas kernels for 0% -> 0%
where the time goes in v1:
time: 147 us
  Pallas kernels  139 us (95%)
  local copies, waits for them, and re-layouts  7.94 us (5%)
    pallas_call x1, Pallas kernels, local(): pl.pallas_call(functools.partial(kernel, chunks), out_shape=jax.ShapeDtyp...  139 us
    unnamed x17, local copies, waits for them, and re-layouts  7.94 us

profile of v1, /device:TPU:1, one launch (start us, length us, event | category | flops | bytes accessed | tf_op | source)
XLA Modules:
  0.0 146.6 jit_solution(10690142902413264263)
XLA Ops:
  0.0 0.0 copy-start
  0.0 1.6 %copy-done = bf16[1,2880,360]{1,2,0:T(8,128)(2,1)S(1)} copy-done((bf16[1,2880,360]{1,2,0:T(8,128)(2,1)S(1)}, bf16[1,2880,360]{1,2,0:T(8,128)(2,1)}, u32[]{:S(2)}) %copy-start) | copy-done | bytes 2073624
  1.6 0.0 copy-start.1
  1.6 0.9 copy-done.1
  2.5 0.0 copy-start.2
  2.5 0.9 copy-done.2
  3.4 0.0 copy-start.3
  3.4 0.9 copy-done.3
  4.3 0.0 copy-start.4
  4.3 0.8 copy-done.4
  5.1 0.0 copy-start.5
  5.1 0.8 copy-done.5
  5.9 0.0 copy-start.6
  5.9 0.7 copy-done.6
  6.6 0.0 copy-start.7
  6.6 0.7 copy-done.7
  7.3 138.7 %shard_map.91 = bf16[720,128]{1,0:T(8,128)(2,1)S(1)} custom-call(s32[4,128]{1,0:T(4,128)S(1)} %bitcast.20, s32[4,128]{1,0:T(4,128)S(1)} %bitcast.21, bf16[720,128]{1,0:T(8,128)(2,1)S(1)} %bitcast.15, bf16[1,360,2880]{2,1,0:T(8,128)(2,1)S(1)} %bitcast.14, bf16[1,360,2880]{2,1,0:T(8,128)(2,1)} %wdn_hbm.1, bf16[16,2880]{1,0:T(8,128)(2,1)S(1)} %bitcast.17, ...), custom_call_target="tpu_custom_call" | custom-call | flops 8000000000 | bytes 6000000 | tf_op jit(solution)/shard_map/pallas_call | solution.py:346
  145.9 0.7 copy.11
Async XLA Ops:
  0.0 1.6 %copy-start = (bf16[1,2880,360]{1,2,0:T(8,128)(2,1)S(1)}, bf16[1,2880,360]{1,2,0:T(8,128)(2,1)}, u32[]{:S(2)}) copy-start(bf16[1,2880,360]{1,2,0:T(8,128)(2,1)} %param.12) | copy-start | bytes 6220804
  1.6 0.9 copy-start.1
  2.5 0.9 copy-start.2
  3.4 0.9 copy-start.3
  4.3 0.8 copy-start.4
  5.1 0.8 copy-start.5
  5.9 0.7 copy-start.6
  6.6 0.7 copy-start.7

commit v2 on v1

v2 whole, which is shorter than its diff:
```python
import functools

import jax
import jax.numpy as jnp
from jax import lax
from jax.experimental import pallas as pl
from jax.experimental.pallas import tpu as pltpu
from jax.sharding import PartitionSpec as P

NZ, NY, NX = 8, 8, 4
CAP = 5
SLOTS = 2 * CAP
LANES = 128
BF16, F32, I32 = jnp.bfloat16, jnp.float32, jnp.int32

NN = (((1,), (0,)), ((), ()))
NT = (((1,), (1,)), ((), ()))
TN = (((0,), (0,)), ((), ()))

(OUT_1, OUT_2, OUT_RIGHT, OUT_LEFT, OUT_RIGHT2, OUT_LEFT2, SUM_RIGHT, SUM_LEFT, SUM_RIGHT2, SUM_LEFT2,
 BACK_1, BACK_2, MERGE, KINDS) = range(14)
TOK, META, UP_IN, DOWN_OUT = range(4)


def dot(a, b, dims):
    return lax.dot_general(a, b, dims, preferred_element_type=F32)


def kernel(chunks, routes_hbm, gates_hbm, tok_hbm, wup_hbm, wdn_hbm, aup_hbm, bup_hbm, adn_hbm, bdn_hbm, out_ref,
           routes_ref, gates_ref, tok_ref, aup_ref, bup_ref, adn_ref, bdn_ref, tok2, meta, sel, selz, gain, gainz, perm, wraw, wdraw, afull, bfull, w1, w2,
           ysend, yrecv, zsend, late, gath, acc, hid, part, half_l, half_r, full_l, full_r,
           total, esend, zback, yback, rback, msend, mrecv, own,
           send_sem, recv_sem, send_once, recv_once, local_sem):
    expert, x = lax.axis_index("expert"), lax.axis_index("tensor")
    z, y, core = expert // (2 * NY), (expert // 2) % NY, expert % 2
    right, left, across = (x + 1) % NX, (x + NX - 1) % NX, (x + 2) % NX
    quarter, tokens = tok_ref.shape
    hidden = bup_ref.shape[1]
    rank = bup_ref.shape[0]
    part_rank = aup_ref.shape[0]
    code_at = w1.shape[1] - rank
    ygroup = SLOTS * NZ
    rows = ygroup * NY
    half = rows // 2
    last = quarter - (chunks - 1) * LANES

    def at(zz, yy, cc):
        return {"expert": (zz * NY + yy) * 2 + cc}

    sibling = at(z, y, 1 - core)

    def send(src, dst, kind, k, device):
        pltpu.make_async_remote_copy(
            src_ref=src, dst_ref=dst, send_sem=send_sem.at[kind, k], recv_sem=recv_sem.at[kind, k],
            device_id=device, device_id_type=pl.DeviceIdType.MESH).start()

    def arrived(ref, kind, k):
        pltpu.make_async_copy(ref, ref, recv_sem.at[kind, k]).wait()

    def sent(ref, kind, k):
        pltpu.make_async_copy(ref, ref, send_sem.at[kind, k]).wait()

    def send_one(src, dst, which, device):
        pltpu.make_async_remote_copy(
            src_ref=src, dst_ref=dst, send_sem=send_once.at[which], recv_sem=recv_once.at[which],
            device_id=device, device_id_type=pl.DeviceIdType.MESH).start()

    loads = [pltpu.make_async_copy(hbm, ref, local_sem.at[i]) for i, (hbm, ref) in enumerate((
        (routes_hbm, routes_ref), (gates_hbm, gates_ref), (tok_hbm, tok_ref), (aup_hbm, aup_ref), (bdn_hbm, bdn_ref),
        (wup_hbm, wraw), (wdn_hbm, wdraw), (bup_hbm, bup_ref), (adn_hbm, adn_ref)))]
    for load in loads:
        load.start()
    load_up, load_down, load_bup, load_adn = loads[5:]

    barrier = pltpu.get_barrier_semaphore()

    def greet(device):
        pl.semaphore_signal(barrier, inc=1, device_id=device, device_id_type=pl.DeviceIdType.MESH)

    greet(sibling)

    @pl.loop(1, NY)
    def _(j):
        greet(at(z, (y + j) % NY, core))

    @pl.loop(1, NZ)
    def _(j):
        greet(at((z + j) % NZ, y, core))

    @pl.loop(1, NX)
    def _(j):
        greet({"tensor": (x + j) % NX})

    for load in loads[:2]:
        load.wait()
    meta[0, 0:4, :] = routes_ref[...]
    meta[0, 4:8, :] = gates_ref[...]

    before = (lax.broadcasted_iota(I32, (tokens, tokens), 0)
              < lax.broadcasted_iota(I32, (tokens, tokens), 1)).astype(F32).astype(BF16)
    slot_row = lax.broadcasted_iota(I32, (CAP * NZ, tokens), 0)
    slot_of = (slot_row // NZ).astype(F32)
    first_id = (slot_row % NZ) * (2 * NY) + core
    none = jnp.zeros((CAP * NZ, tokens), F32)

    def picks(src):
        for yy in range(NY):
            hit = jnp.zeros((CAP * NZ, tokens), F32)
            for k in range(4):
                hit = jnp.where(meta[src, k:k + 1, :] == first_id + 2 * yy, 1.0, hit)
            position = dot(hit.astype(BF16), before, NN)
            yield jnp.where(position == slot_of, hit, 0.0)

    def both(mine, theirs):
        return jnp.concatenate([jnp.concatenate([mine, none], axis=1),
                                jnp.concatenate([none, theirs], axis=1)], axis=0).astype(BF16)

    row = lax.broadcasted_iota(I32, (ygroup, rows), 0)
    column = lax.broadcasted_iota(I32, (ygroup, rows), 1)
    source = (row % NZ) * ygroup + (row // NZ) * NZ
    for a in range(NY):
        perm[a * ygroup:(a + 1) * ygroup, :] = (column == source + a).astype(F32).astype(BF16)
    own_picks = list(picks(0))
    for load in loads[2:5]:
        load.wait()

    pl.semaphore_wait(barrier, NY + NZ + NX - 2)

    send_one(meta.at[0], meta.at[1], META, sibling)
    send_one(tok_ref, tok2.at[0:quarter, tokens:2 * tokens], TOK, sibling)

    @pl.loop(1, NX)
    def _(j):
        mine = pl.ds(pl.multiple_of(x * part_rank, part_rank), part_rank)
        send_one(aup_ref, afull.at[mine], UP_IN, {"tensor": (x + j) % NX})
        send_one(bdn_ref, bfull.at[x], DOWN_OUT, {"tensor": (x + j) % NX})

    tok2[0:quarter, 0:tokens] = tok_ref[...]
    tok2[quarter:, :] = jnp.zeros_like(tok2[quarter:, :])

    pltpu.make_async_copy(meta.at[0], meta.at[1], recv_once.at[META]).wait()
    for yy, (mine, theirs) in enumerate(zip(own_picks, picks(1))):
        sel[yy * ygroup:(yy + 1) * ygroup, :] = both(mine, theirs)

    def prepare():
        acc[...] = jnp.zeros_like(acc)
        hid[...] = jnp.zeros_like(hid)
        afull[pl.ds(pl.multiple_of(x * part_rank, part_rank), part_rank), :] = aup_ref[...]
        bfull[x] = bdn_ref[...]

    def weigh():
        for yy in range(NY):
            block = slice(yy * ygroup, (yy + 1) * ygroup)
            highs, lows = [], []
            for src in range(2):
                gate = jnp.zeros((CAP * NZ, tokens), I32)
                for k in range(4):
                    same = meta[src, k:k + 1, :] == first_id + 2 * yy
                    gate = jnp.where(same, meta[src, 4 + k:5 + k, :], gate)
                highs.append((gate >> 8).astype(F32) * (1.0 / 256.0))
                lows.append((gate & 255).astype(F32) * (1.0 / 65536.0))
            pick = sel[block, :]
            gain[block, 0:2 * tokens] = pick * both(*highs)
            gain[block, 2 * tokens:] = pick * both(*lows)
        gainz[...] = dot(perm[...], gain[...], NN).astype(BF16)

    pltpu.make_async_copy(tok_ref, tok2.at[0:quarter, tokens:2 * tokens], recv_once.at[TOK]).wait()

    place = (y, z)

    def block(i):
        return pl.ds(pl.multiple_of(i * ygroup, 16), ygroup)

    def scatter(src, dst, axis, kind, k):
        @pl.loop(1, NY)
        def _(j):
            i = (place[axis] + j) % NY
            send(src.at[block(i)], dst.at[block(place[axis])], kind, k, at(z, i, core) if axis == 0 else at(i, y, core))

        dst[block(place[axis]), :] = src[block(place[axis]), :]

    def choose(k, p):
        feats = pl.ds(pl.multiple_of(k * LANES, LANES), LANES)
        ysend[k] = dot((sel, selz)[p][...], tok2[feats, :], NT).astype(BF16)
        scatter(ysend.at[k], yrecv.at[k], p, OUT_1, k)

    def pass_on(k, p):
        arrived(yrecv.at[k, 0:rows - ygroup], OUT_1, k)
        zsend[k] = dot(perm[...], yrecv[k], NN).astype(BF16)
        scatter(zsend.at[k], late.at[k] if p else gath.at[k, x], 1 - p, OUT_2, k)

    def span(h, scale=1):
        count = rows // scale
        return slice(0, count) if h is None else slice(h * count // 2, (h + 1) * count // 2)

    def slot(k, h):
        return k + chunks if h == 1 else k

    def ends(h):
        whole = span(h)
        middle = (whole.start + whole.stop) // 2
        return slice(whole.start, middle), slice(middle, whole.stop)

    def spread(k, p, h=None):
        if h != 1:
            arrived(yrecv.at[k, 0:rows - ygroup], OUT_2, k)
            if p:
                gath[k, x] = dot(perm[...], late[k], NN).astype(BF16)
        mine = gath.at[k, x, span(h)]
        send(mine, mine, OUT_RIGHT, slot(k, h), {"tensor": right})
        send(mine, mine, OUT_LEFT, slot(k, h), {"tensor": left})

    def forward(k, h=None):
        top, bottom = ends(h)
        arrived(gath.at[k, left, span(h)], OUT_RIGHT, slot(k, h))
        send(gath.at[k, left, top], gath.at[k, left, top], OUT_RIGHT2, slot(k, h), {"tensor": right})
        arrived(gath.at[k, right, span(h)], OUT_LEFT, slot(k, h))
        send(gath.at[k, right, bottom], gath.at[k, right, bottom], OUT_LEFT2, slot(k, h), {"tensor": left})

    def multiply(k, h=None):
        top, bottom = ends(h)
        arrived(gath.at[k, across, top], OUT_RIGHT2, slot(k, h))
        arrived(gath.at[k, across, bottom], OUT_LEFT2, slot(k, h))
        lhs = jnp.concatenate([gath[k, q, span(h), :] for q in range(NX)], axis=1)
        acc[span(h), :] += dot(lhs, w1[k], NT)

    def arrange(raw, weights):
        for k in range(chunks):
            width = min(LANES, quarter - k * LANES)
            for q in range(NX):
                first = q * quarter + k * LANES
                weights[k, 0:hidden, q * LANES:q * LANES + width] = raw[0, :, first:first + width]

    def arrange_up():
        load_up.wait()
        w1[...] = jnp.zeros_like(w1)
        arrange(wraw, w1)

    def arrange_down():
        load_down.wait()
        w2[...] = jnp.zeros_like(w2)
        arrange(wdraw, w2)

    def arrange_adapters():
        pltpu.make_async_copy(afull.at[0:(NX - 1) * part_rank], afull.at[0:(NX - 1) * part_rank],
                              recv_once.at[UP_IN]).wait()
        pltpu.make_async_copy(bfull.at[0:NX - 1], bfull.at[0:NX - 1], recv_once.at[DOWN_OUT]).wait()
        for k in range(chunks):
            width = min(LANES, quarter - k * LANES)
            for q in range(NX):
                first = q * quarter + k * LANES
                w1[k, code_at:, q * LANES:q * LANES + width] = afull[:, first:first + width]
                w2[k, code_at:, q * LANES:q * LANES + width] = bfull[q, :, k * LANES:k * LANES + width]

    pairs = chunks // 2

    def step(tick, stage, delay, parity, *more):
        pair = tick - delay

        @pl.when((pair >= 0) & (pair < pairs))
        def _():
            stage(2 * pair + parity, *more)

    choose(0, 0)
    selz[...] = dot(perm[...], sel[...], NN).astype(BF16)
    choose(1, 1)
    if pairs > 1:
        choose(2, 0)
        choose(3, 1)
    prepare()
    arrange_up()

    @pl.loop(0, pairs)
    def _(t):
        step(t, pass_on, 0, 0, 0)
        step(t, pass_on, 0, 1, 1)
        step(t, choose, -2, 0, 0)
        step(t, choose, -2, 1, 1)

        @pl.when(t == 0)
        def _():
            weigh()

        step(t, forward, 2, 0)
        step(t, spread, 1, 0, 0)
        step(t, spread, 1, 1, 1)

        @pl.when(t == min(1, pairs - 1))
        def _():
            arrange_down()
            arrange_adapters()

        step(t, forward, 2, 1)
        step(t, multiply, 3, 1)
        step(t, multiply, 2, 0)

    load_bup.wait()
    load_adn.wait()

    def activate(h):
        codes = acc[span(h), code_at:].astype(BF16)
        upward = acc[span(h), 0:hidden] + 0.5 * dot(codes, bup_ref[...], NN)
        units = (upward * jax.nn.sigmoid(1.702 * upward)).astype(BF16)
        hid[span(h), 0:hidden] = units
        hid[span(h), code_at:] = (0.5 * dot(units, adn_ref[...], NT)).astype(BF16)

    def partial(k, h=None):
        top, bottom = ends(h)
        product = dot(hid[span(h), :], w2[k], NN).astype(BF16)
        for q in range(NX):
            part[k, q, span(h), :] = product[:, q * LANES:(q + 1) * LANES]
        send(part.at[k, across, top], half_l.at[k, span(h, 2)], SUM_RIGHT, slot(k, h), {"tensor": right})
        send(part.at[k, across, bottom], half_r.at[k, span(h, 2)], SUM_LEFT, slot(k, h), {"tensor": left})

    def add_half(k, h=None):
        top, bottom = ends(h)
        half_of = span(h, 2)
        arrived(half_l.at[k, half_of], SUM_RIGHT, slot(k, h))
        part[k, right, top, :] = (part[k, right, top, :].astype(F32) + half_l[k, half_of, :].astype(F32)).astype(BF16)
        send(part.at[k, right, span(h)], full_l.at[k, span(h)], SUM_RIGHT2, slot(k, h), {"tensor": right})
        arrived(half_r.at[k, half_of], SUM_LEFT, slot(k, h))
        part[k, left, bottom, :] = (part[k, left, bottom, :].astype(F32)
                                    + half_r[k, half_of, :].astype(F32)).astype(BF16)
        send(part.at[k, left, span(h)], full_r.at[k, span(h)], SUM_LEFT2, slot(k, h), {"tensor": left})

    def add_full(k, p, h=None):
        where = span(h)
        arrived(full_l.at[k, where], SUM_RIGHT2, slot(k, h))
        arrived(full_r.at[k, where], SUM_LEFT2, slot(k, h))
        total[where, :] = (part[k, x, where, :].astype(F32) + full_l[k, where, :].astype(F32)
                           + full_r[k, where, :].astype(F32)).astype(BF16)
        if h != 0:
            esend[k] = dot(perm[...], total[...], NN).astype(BF16) if p else total[...]
            scatter(esend.at[k], zback.at[k], 1 - p, BACK_1, k)

    def pass_back(k, p):
        arrived(zback.at[k, 0:rows - ygroup], BACK_1, k)
        yback[k] = dot(perm[...], zback[k], NN).astype(BF16)
        scatter(yback.at[k], rback.at[k], p, BACK_2, k)

    def mix(k, p):
        arrived(rback.at[k, 0:rows - ygroup], BACK_2, k)
        both_parts = dot(rback[k], (gain, gainz)[p][...], TN)
        mixed = both_parts[:, 0:2 * tokens] + both_parts[:, 2 * tokens:]
        own[k] = mixed[:, 0:tokens]
        msend[k] = mixed[:, tokens:]
        send(msend.at[k], mrecv.at[k], MERGE, k, sibling)

    def finish(k):
        arrived(mrecv.at[k], MERGE, k)
        own[k] = own[k] + mrecv[k]

    end = chunks - 2
    more = pairs > 1
    if more:
        forward(end - 2)
    spread(end, 0, 0)
    spread(end + 1, 1, 0)
    if more:
        forward(end - 1)
    spread(end, 0, 1)
    spread(end + 1, 1, 1)
    if pairs > 2:
        multiply(end - 3)
    if more:
        multiply(end - 2)
    forward(end, 0)
    forward(end + 1, 0)
    if more:
        multiply(end - 1)
    forward(end, 1)
    forward(end + 1, 1)
    for h in range(2):
        multiply(end, h)
        multiply(end + 1, h)
        activate(h)
        partial(0, h)
        partial(1, h)
    for h in range(2):
        add_half(0, h)
        add_half(1, h)
        if more:
            partial(2 + h)
    if more:
        add_half(2)
        if pairs > 2:
            partial(4)
    add_full(0, 0, 0)
    add_full(0, 0, 1)
    if more:
        add_half(3)
        if pairs > 2:
            partial(5)
    add_full(1, 1, 0)
    add_full(1, 1, 1)

    @pl.loop(2, pairs + 4)
    def _(t):
        for p in range(2):
            step(t, add_half, 0, p)
            step(t, partial, -1, p)
            step(t, add_full, 1, p, p)
        step(t, pass_back, 2, 0, 0)
        step(t, pass_back, 2, 1, 1)
        step(t, mix, 3, 0, 0)
        step(t, mix, 3, 1, 1)
        step(t, finish, 4, 0)
        step(t, finish, 4, 1)

    for k in range(chunks):
        width = min(LANES, quarter - k * LANES)
        out_ref[k * LANES:k * LANES + width, :] = own[k, 0:width, :].astype(BF16)

    @pl.loop(0, chunks)
    def _(k):
        sent(ysend.at[k, 0:rows - ygroup], OUT_1, k)
        sent(zsend.at[k, 0:rows - ygroup], OUT_2, k)
        sent(esend.at[k, 0:rows - ygroup], BACK_1, k)
        sent(yback.at[k, 0:rows - ygroup], BACK_2, k)
        sent(msend.at[k], MERGE, k)

    for k in range(chunks):
        for h in (0, 1) if k >= end else (None,):
            top, bottom = ends(h)
            sent(gath.at[k, 0, span(h)], OUT_RIGHT, slot(k, h))
            sent(gath.at[k, 0, span(h)], OUT_LEFT, slot(k, h))
            sent(gath.at[k, 0, top], OUT_RIGHT2, slot(k, h))
            sent(gath.at[k, 0, bottom], OUT_LEFT2, slot(k, h))
        for h in (0, 1) if k < 2 else (None,):
            sent(half_l.at[k, span(h, 2)], SUM_RIGHT, slot(k, h))
            sent(half_r.at[k, span(h, 2)], SUM_LEFT, slot(k, h))
            sent(full_l.at[k, span(h)], SUM_RIGHT2, slot(k, h))
            sent(full_r.at[k, span(h)], SUM_LEFT2, slot(k, h))

    pltpu.make_async_copy(meta.at[0], meta.at[1], send_once.at[META]).wait()
    pltpu.make_async_copy(tok_ref, tok2.at[0:quarter, tokens:2 * tokens], send_once.at[TOK]).wait()
    pltpu.make_async_copy(afull.at[0:(NX - 1) * part_rank], afull.at[0:(NX - 1) * part_rank],
                          send_once.at[UP_IN]).wait()
    pltpu.make_async_copy(bfull.at[0:NX - 1], bfull.at[0:NX - 1], send_once.at[DOWN_OUT]).wait()


def local(tokens, routes, gates, wup, wdn, aup, bup, adn, bdn):
    count, quarter = tokens.shape
    hidden, rank = wup.shape[2], bup.shape[1]
    part_rank = aup.shape[2]
    chunks = -(-quarter // LANES)
    rows = SLOTS * NY * NZ
    inner = -(-hidden // LANES) * LANES + rank
    grid = (chunks, rows, LANES)
    vmem, hbm = pl.BlockSpec(memory_space=pltpu.VMEM), pl.BlockSpec(memory_space=pl.ANY)
    out = pl.pallas_call(
        functools.partial(kernel, chunks),
        out_shape=jax.ShapeDtypeStruct((quarter, count), BF16),
        in_specs=[hbm] * 9,
        out_specs=vmem,
        scratch_shapes=[
            pltpu.VMEM((4, count), I32),
            pltpu.VMEM((4, count), I32),
            pltpu.VMEM((quarter, count), BF16),
            pltpu.VMEM((part_rank, NX * quarter), BF16),
            pltpu.VMEM((rank, hidden), BF16),
            pltpu.VMEM((rank, hidden), BF16),
            pltpu.VMEM((rank, quarter), BF16),
            pltpu.VMEM((chunks * LANES, 2 * count), BF16),
            pltpu.VMEM((2, 8, count), I32),
            pltpu.VMEM((rows, 2 * count), BF16),
            pltpu.VMEM((rows, 2 * count), BF16),
            pltpu.VMEM((rows, 4 * count), BF16),
            pltpu.VMEM((rows, 4 * count), BF16),
            pltpu.VMEM((rows, rows), BF16),
            pltpu.VMEM((1, hidden, NX * quarter), BF16),
            pltpu.VMEM((1, hidden, NX * quarter), BF16),
            pltpu.VMEM((rank, NX * quarter), BF16),
            pltpu.VMEM((NX, rank, quarter), BF16),
            pltpu.VMEM((chunks, inner, NX * LANES), BF16),
            pltpu.VMEM((chunks, inner, NX * LANES), BF16),
            pltpu.VMEM(grid, BF16),
            pltpu.VMEM(grid, BF16),
            pltpu.VMEM(grid, BF16),
            pltpu.VMEM(grid, BF16),
            pltpu.VMEM((chunks, NX, rows, LANES), BF16),
            pltpu.VMEM((rows, inner), F32),
            pltpu.VMEM((rows, inner), BF16),
            pltpu.VMEM((chunks, NX, rows, LANES), BF16),
            pltpu.VMEM((chunks, rows // 2, LANES), BF16),
            pltpu.VMEM((chunks, rows // 2, LANES), BF16),
            pltpu.VMEM(grid, BF16),
            pltpu.VMEM(grid, BF16),
            pltpu.VMEM((rows, LANES), BF16),
            pltpu.VMEM(grid, BF16),
            pltpu.VMEM(grid, BF16),
            pltpu.VMEM(grid, BF16),
            pltpu.VMEM(grid, BF16),
            pltpu.VMEM((chunks, LANES, count), F32),
            pltpu.VMEM((chunks, LANES, count), F32),
            pltpu.VMEM((chunks, LANES, count), F32),
            pltpu.SemaphoreType.DMA((KINDS, 2 * chunks)),
            pltpu.SemaphoreType.DMA((KINDS, 2 * chunks)),
            pltpu.SemaphoreType.DMA((4,)),
            pltpu.SemaphoreType.DMA((4,)),
            pltpu.SemaphoreType.DMA((9,)),
        ],
        compiler_params=pltpu.CompilerParams(
            collective_id=0, has_side_effects=True, vmem_limit_bytes=60 * 1024 * 1024),
        cost_estimate=pl.CostEstimate(flops=8 * 10**9, bytes_accessed=6 * 10**6, transcendentals=0),
    )(routes.T, gates.T, tokens.T, jnp.swapaxes(wup, 1, 2), wdn, aup[0].T, bup[0], adn[0].T, bdn[0])
    return out.T


def solution(mesh):
    return jax.shard_map(
        local,
        mesh=mesh,
        in_specs=(
            P("expert", "tensor"),
            P("expert", None),
            P("expert", None),
            P("expert", None, "tensor"),
            P("expert", "tensor", None),
            P("expert", None, "tensor"),
            P("expert", None, "tensor"),
            P("expert", "tensor", None),
            P("expert", None, "tensor"),
        ),
        out_specs=P("expert", "tensor"),
        check_vma=False,
    )
```

time: 147 us -> 120 us (0.82)
  Pallas kernels: 139 us -> 119 us
  local copies, waits for them, and re-layouts: 7.94 us -> 1.61 us
    pallas_call x1, Pallas kernels: 139 us -> 119 us  [local(): pl.pallas_call(functools.partial(kernel, chunks), out_shape=jax.ShapeDtyp...]
    unnamed x17 -> x1, local copies, waits for them, and re-layouts: 7.94 us -> 1.61 us
where the time goes in v2:
time: 120 us
  Pallas kernels  119 us (99%)
  local copies, waits for them, and re-layouts  1.61 us (1%)
    pallas_call x1, Pallas kernels, local(): pl.pallas_call(functools.partial(kernel, chunks), out_shape=jax.ShapeDtyp...  119 us

profile of v2, /device:TPU:1, one launch (start us, length us, event | category | flops | bytes accessed | tf_op | source)
XLA Modules:
  0.0 120.2 jit_solution(8790733498388421657)
XLA Ops:
  0.0 118.6 %shard_map.91 = bf16[720,128]{1,0:T(8,128)(2,1)} custom-call(s32[4,128]{1,0:T(4,128)} %bitcast.20, s32[4,128]{1,0:T(4,128)} %bitcast.21, bf16[720,128]{1,0:T(8,128)(2,1)} %bitcast.15, bf16[1,360,2880]{2,1,0:T(8,128)(2,1)} %bitcast.14, bf16[1,360,2880]{2,1,0:T(8,128)(2,1)} %wdn_hbm.1, bf16[16,2880]{1,0:T(8,128)(2,1)} %bitcast.17, bf16[64,360]{1,0:T(8,128)(2,1)} %bitcast.18, ...), custom_call_target="tpu_custom_call" | custom-call | flops 8000000000 | bytes 6000000 | tf_op jit(solution)/shard_map/pallas_call | solution.py:451
  118.6 1.6 %copy.11 = bf16[128,720]{0,1:T(8,128)(2,1)} copy(bf16[128,720]{0,1:T(8,128)(2,1)} %bitcast.13) | data formatting | bytes 368640

commit v3 on v2

--- a/solution.py
+++ b/solution.py
@@ -18,8 +18,8 @@
 TN = (((0,), (0,)), ((), ()))
 
 (OUT_1, OUT_2, OUT_RIGHT, OUT_LEFT, OUT_RIGHT2, OUT_LEFT2, SUM_RIGHT, SUM_LEFT, SUM_RIGHT2, SUM_LEFT2,
- BACK_1, BACK_2, MERGE, KINDS) = range(14)
-TOK, META, UP_IN, DOWN_OUT = range(4)
+ BACK_1, BACK_2, KINDS) = range(13)
+UP_IN, DOWN_OUT = range(2)
 
 
 def dot(a, b, dims):
@@ -27,9 +27,9 @@
 
 
 def kernel(chunks, routes_hbm, gates_hbm, tok_hbm, wup_hbm, wdn_hbm, aup_hbm, bup_hbm, adn_hbm, bdn_hbm, out_ref,
-           routes_ref, gates_ref, tok_ref, aup_ref, bup_ref, adn_ref, bdn_ref, tok2, meta, sel, selz, gain, gainz, perm, wraw, wdraw, afull, bfull, w1, w2,
+           routes_ref, gates_ref, tok_ref, aup_ref, bup_ref, adn_ref, bdn_ref, tok2, sel, selz, gain, gainz, perm, merge, split, wraw, wdraw, afull, bfull, w1, w2,
            ysend, yrecv, zsend, late, gath, acc, hid, part, half_l, half_r, full_l, full_r,
-           total, esend, zback, yback, rback, msend, mrecv, own,
+           total, esend, zback, yback, rback, own,
            send_sem, recv_sem, send_once, recv_once, local_sem):
     expert, x = lax.axis_index("expert"), lax.axis_index("tensor")
     z, y, core = expert // (2 * NY), (expert // 2) % NY, expert % 2
@@ -42,12 +42,13 @@
     ygroup = SLOTS * NZ
     rows = ygroup * NY
     half = rows // 2
+    filled = CAP * NZ
+    padded = -(-filled // 16) * 16
+    spread_rows = 2 * NY * padded
     last = quarter - (chunks - 1) * LANES
 
     def at(zz, yy, cc):
         return {"expert": (zz * NY + yy) * 2 + cc}
-
-    sibling = at(z, y, 1 - core)
 
     def send(src, dst, kind, k, device):
         pltpu.make_async_remote_copy(
@@ -77,70 +78,101 @@
     def greet(device):
         pl.semaphore_signal(barrier, inc=1, device_id=device, device_id_type=pl.DeviceIdType.MESH)
 
-    greet(sibling)
+    greet(at(z, y, 1 - core))
 
     @pl.loop(1, NY)
     def _(j):
-        greet(at(z, (y + j) % NY, core))
+        for cc in range(2):
+            greet(at(z, (y + j) % NY, cc))
 
     @pl.loop(1, NZ)
     def _(j):
-        greet(at((z + j) % NZ, y, core))
+        for cc in range(2):
+            greet(at((z + j) % NZ, y, cc))
 
     @pl.loop(1, NX)
     def _(j):
         greet({"tensor": (x + j) % NX})
 
-    for load in loads[:2]:
+    for load in loads[:3]:
         load.wait()
-    meta[0, 0:4, :] = routes_ref[...]
-    meta[0, 4:8, :] = gates_ref[...]
+    tok2[0:quarter, :] = tok_ref[...]
+    tok2[quarter:, :] = jnp.zeros_like(tok2[quarter:, :])
 
     before = (lax.broadcasted_iota(I32, (tokens, tokens), 0)
               < lax.broadcasted_iota(I32, (tokens, tokens), 1)).astype(F32).astype(BF16)
-    slot_row = lax.broadcasted_iota(I32, (CAP * NZ, tokens), 0)
+    slot_row = lax.broadcasted_iota(I32, (filled, tokens), 0)
     slot_of = (slot_row // NZ).astype(F32)
-    first_id = (slot_row % NZ) * (2 * NY) + core
-    none = jnp.zeros((CAP * NZ, tokens), F32)
-
-    def picks(src):
-        for yy in range(NY):
-            hit = jnp.zeros((CAP * NZ, tokens), F32)
-            for k in range(4):
-                hit = jnp.where(meta[src, k:k + 1, :] == first_id + 2 * yy, 1.0, hit)
-            position = dot(hit.astype(BF16), before, NN)
-            yield jnp.where(position == slot_of, hit, 0.0)
-
-    def both(mine, theirs):
-        return jnp.concatenate([jnp.concatenate([mine, none], axis=1),
-                                jnp.concatenate([none, theirs], axis=1)], axis=0).astype(BF16)
-
-    row = lax.broadcasted_iota(I32, (ygroup, rows), 0)
-    column = lax.broadcasted_iota(I32, (ygroup, rows), 1)
-    source = (row % NZ) * ygroup + (row // NZ) * NZ
-    for a in range(NY):
-        perm[a * ygroup:(a + 1) * ygroup, :] = (column == source + a).astype(F32).astype(BF16)
-    own_picks = list(picks(0))
-    for load in loads[2:5]:
+    none = jnp.zeros((padded - filled, tokens), F32)
+
+    def expert_ids(p, i, cc):
+        return (slot_row % NZ) * (2 if p else 2 * NY) + (i * (2 * NY if p else 2) + cc)
+
+    def fill(table, p):
+        for i in range(NY):
+            for cc in range(2):
+                hit = jnp.zeros((filled, tokens), F32)
+                for k in range(4):
+                    hit = jnp.where(routes_ref[k:k + 1, :] == expert_ids(p, i, cc), 1.0, hit)
+                position = dot(hit.astype(BF16), before, NN)
+                pick = jnp.where(position == slot_of, hit, 0.0)
+                first = (2 * i + cc) * padded
+                table[first:first + padded, :] = jnp.concatenate([pick, none], axis=0).astype(BF16)
+
+    def weigh():
+        for p, chosen, table in ((0, sel, gain), (1, selz, gainz)):
+            for i in range(NY):
+                for cc in range(2):
+                    gate = jnp.zeros((filled, tokens), I32)
+                    for k in range(4):
+                        gate = jnp.where(routes_ref[k:k + 1, :] == expert_ids(p, i, cc), gates_ref[k:k + 1, :], gate)
+                    first = (2 * i + cc) * padded
+                    pick = chosen[first:first + padded, :]
+                    high = (gate >> 8).astype(F32) * (1.0 / 256.0)
+                    low = (gate & 255).astype(F32) * (1.0 / 65536.0)
+                    table[first:first + padded, 0:tokens] = pick * jnp.concatenate([high, none], axis=0).astype(BF16)
+                    table[first:first + padded, tokens:] = pick * jnp.concatenate([low, none], axis=0).astype(BF16)
+
+    def order_merge():
+        row = lax.broadcasted_iota(I32, (ygroup, spread_rows), 0)
+        column = lax.broadcasted_iota(I32, (ygroup, spread_rows), 1)
+        both_slot = row // NZ
+        source = ((row % NZ) * 2 + both_slot // CAP) * padded + (both_slot % CAP) * NZ
+        for a in range(NY):
+            merge[a * ygroup:(a + 1) * ygroup, :] = (column == source + a).astype(F32).astype(BF16)
+
+    def order_blocks():
+        row = lax.broadcasted_iota(I32, (ygroup, rows), 0)
+        column = lax.broadcasted_iota(I32, (ygroup, rows), 1)
+        source = (row % NZ) * ygroup + (row // NZ) * NZ
+        for a in range(NY):
+            perm[a * ygroup:(a + 1) * ygroup, :] = (column == source + a).astype(F32).astype(BF16)
+
+    def order_split():
+        row = lax.broadcasted_iota(I32, (padded, rows), 0)
+        column = lax.broadcasted_iota(I32, (padded, rows), 1)
+        target = jnp.where(row < filled, (row % NZ) * ygroup + (row // NZ) * NZ, rows)
+        for i in range(NY):
+            for cc in range(2):
+                first = (2 * i + cc) * padded
+                split[first:first + padded, :] = (column == target + (cc * CAP * NZ + i)).astype(F32).astype(BF16)
+
+    fill(sel, 0)
+    fill(selz, 1)
+    order_merge()
+    ysend[0] = dot(sel[...], tok2[0:LANES, :], NT).astype(BF16)
+    for load in loads[3:5]:
         load.wait()
 
-    pl.semaphore_wait(barrier, NY + NZ + NX - 2)
-
-    send_one(meta.at[0], meta.at[1], META, sibling)
-    send_one(tok_ref, tok2.at[0:quarter, tokens:2 * tokens], TOK, sibling)
-
-    @pl.loop(1, NX)
-    def _(j):
+    pl.semaphore_wait(barrier, 2 * NY + 2 * NZ + NX - 4)
+
+    def exchange():
         mine = pl.ds(pl.multiple_of(x * part_rank, part_rank), part_rank)
-        send_one(aup_ref, afull.at[mine], UP_IN, {"tensor": (x + j) % NX})
-        send_one(bdn_ref, bfull.at[x], DOWN_OUT, {"tensor": (x + j) % NX})
-
-    tok2[0:quarter, 0:tokens] = tok_ref[...]
-    tok2[quarter:, :] = jnp.zeros_like(tok2[quarter:, :])
-
-    pltpu.make_async_copy(meta.at[0], meta.at[1], recv_once.at[META]).wait()
-    for yy, (mine, theirs) in enumerate(zip(own_picks, picks(1))):
-        sel[yy * ygroup:(yy + 1) * ygroup, :] = both(mine, theirs)
+
+        @pl.loop(1, NX)
+        def _(j):
+            send_one(aup_ref, afull.at[mine], UP_IN, {"tensor": (x + j) % NX})
+            send_one(bdn_ref, bfull.at[x], DOWN_OUT, {"tensor": (x + j) % NX})
 
     def prepare():
         acc[...] = jnp.zeros_like(acc)
@@ -148,45 +180,46 @@
         afull[pl.ds(pl.multiple_of(x * part_rank, part_rank), part_rank), :] = aup_ref[...]
         bfull[x] = bdn_ref[...]
 
-    def weigh():
-        for yy in range(NY):
-            block = slice(yy * ygroup, (yy + 1) * ygroup)
-            highs, lows = [], []
-            for src in range(2):
-                gate = jnp.zeros((CAP * NZ, tokens), I32)
-                for k in range(4):
-                    same = meta[src, k:k + 1, :] == first_id + 2 * yy
-                    gate = jnp.where(same, meta[src, 4 + k:5 + k, :], gate)
-                highs.append((gate >> 8).astype(F32) * (1.0 / 256.0))
-                lows.append((gate & 255).astype(F32) * (1.0 / 65536.0))
-            pick = sel[block, :]
-            gain[block, 0:2 * tokens] = pick * both(*highs)
-            gain[block, 2 * tokens:] = pick * both(*lows)
-        gainz[...] = dot(perm[...], gain[...], NN).astype(BF16)
-
-    pltpu.make_async_copy(tok_ref, tok2.at[0:quarter, tokens:2 * tokens], recv_once.at[TOK]).wait()
-
     place = (y, z)
 
     def block(i):
         return pl.ds(pl.multiple_of(i * ygroup, 16), ygroup)
 
     def scatter(src, dst, axis, kind, k):
-        @pl.loop(1, NY)
-        def _(j):
-            i = (place[axis] + j) % NY
+        @pl.loop(0, NY - 1)
+        def _(n):
+            i = (place[axis] + NY // 2 + (n + 1) // 2 * (1 - 2 * (n % 2))) % NY
             send(src.at[block(i)], dst.at[block(place[axis])], kind, k, at(z, i, core) if axis == 0 else at(i, y, core))
 
         dst[block(place[axis]), :] = src[block(place[axis]), :]
 
-    def choose(k, p):
+    def padded_block(i):
+        return pl.ds(pl.multiple_of(i * padded, 16), padded)
+
+    def scatter_both(src, dst, axis, kind, k):
+        mine = 2 * place[axis] + core
+
+        @pl.loop(0, 2 * NY - 1)
+        def _(n):
+            m = n // 2
+            i = (place[axis] + NY // 2 + (m + 1) // 2 * (1 - 2 * (m % 2))) % NY
+            last_one = n // (2 * NY - 2)
+            i = i + (place[axis] - i) * last_one
+            cc = n % 2 + (1 - core - n % 2) * last_one
+            send(src.at[padded_block(2 * i + cc)], dst.at[padded_block(mine)], kind, k,
+                 at(z, i, cc) if axis == 0 else at(i, y, cc))
+
+        dst[padded_block(mine), :] = src[padded_block(mine), :]
+
+    def choose(k, p, ready=False):
         feats = pl.ds(pl.multiple_of(k * LANES, LANES), LANES)
-        ysend[k] = dot((sel, selz)[p][...], tok2[feats, :], NT).astype(BF16)
-        scatter(ysend.at[k], yrecv.at[k], p, OUT_1, k)
+        if not ready:
+            ysend[k] = dot((sel, selz)[p][...], tok2[feats, :], NT).astype(BF16)
+        scatter_both(ysend.at[k], yrecv.at[k], p, OUT_1, k)
 
     def pass_on(k, p):
-        arrived(yrecv.at[k, 0:rows - ygroup], OUT_1, k)
-        zsend[k] = dot(perm[...], yrecv[k], NN).astype(BF16)
+        arrived(yrecv.at[k, 0:spread_rows - padded], OUT_1, k)
+        zsend[k] = dot(merge[...], yrecv[k], NN).astype(BF16)
         scatter(zsend.at[k], late.at[k] if p else gath.at[k, x], 1 - p, OUT_2, k)
 
     def span(h, scale=1):
@@ -203,7 +236,7 @@
 
     def spread(k, p, h=None):
         if h != 1:
-            arrived(yrecv.at[k, 0:rows - ygroup], OUT_2, k)
+            arrived(late.at[k, 0:rows - ygroup], OUT_2, k)
             if p:
                 gath[k, x] = dot(perm[...], late[k], NN).astype(BF16)
         mine = gath.at[k, x, span(h)]
@@ -261,12 +294,13 @@
         def _():
             stage(2 * pair + parity, *more)
 
-    choose(0, 0)
-    selz[...] = dot(perm[...], sel[...], NN).astype(BF16)
+    choose(0, 0, True)
     choose(1, 1)
+    exchange()
     if pairs > 1:
         choose(2, 0)
         choose(3, 1)
+    order_blocks()
     prepare()
     arrange_up()
 
@@ -280,6 +314,7 @@
         @pl.when(t == 0)
         def _():
             weigh()
+            order_split()
 
         step(t, forward, 2, 0)
         step(t, spread, 1, 0, 0)
@@ -335,20 +370,13 @@
 
     def pass_back(k, p):
         arrived(zback.at[k, 0:rows - ygroup], BACK_1, k)
-        yback[k] = dot(perm[...], zback[k], NN).astype(BF16)
-        scatter(yback.at[k], rback.at[k], p, BACK_2, k)
+        yback[k] = dot(split[...], zback[k], NN).astype(BF16)
+        scatter_both(yback.at[k], rback.at[k], p, BACK_2, k)
 
     def mix(k, p):
-        arrived(rback.at[k, 0:rows - ygroup], BACK_2, k)
+        arrived(rback.at[k, 0:spread_rows - padded], BACK_2, k)
         both_parts = dot(rback[k], (gain, gainz)[p][...], TN)
-        mixed = both_parts[:, 0:2 * tokens] + both_parts[:, 2 * tokens:]
-        own[k] = mixed[:, 0:tokens]
-        msend[k] = mixed[:, tokens:]
-        send(msend.at[k], mrecv.at[k], MERGE, k, sibling)
-
-    def finish(k):
-        arrived(mrecv.at[k], MERGE, k)
-        own[k] = own[k] + mrecv[k]
+        own[k] = both_parts[:, 0:tokens] + both_parts[:, tokens:]
 
     end = chunks - 2
     more = pairs > 1
@@ -394,8 +422,7 @@
     add_full(1, 1, 0)
     add_full(1, 1, 1)
 
-    @pl.loop(2, pairs + 4)
-    def _(t):
+    def tick(t):
         for p in range(2):
             step(t, add_half, 0, p)
             step(t, partial, -1, p)
@@ -404,20 +431,16 @@
         step(t, pass_back, 2, 1, 1)
         step(t, mix, 3, 0, 0)
         step(t, mix, 3, 1, 1)
-        step(t, finish, 4, 0)
-        step(t, finish, 4, 1)
-
-    for k in range(chunks):
-        width = min(LANES, quarter - k * LANES)
-        out_ref[k * LANES:k * LANES + width, :] = own[k, 0:width, :].astype(BF16)
+
+    @pl.loop(2, max(2, pairs + 2))
+    def _(t):
+        tick(t)
 
     @pl.loop(0, chunks)
     def _(k):
-        sent(ysend.at[k, 0:rows - ygroup], OUT_1, k)
+        sent(ysend.at[k, 0:spread_rows - padded], OUT_1, k)
         sent(zsend.at[k, 0:rows - ygroup], OUT_2, k)
         sent(esend.at[k, 0:rows - ygroup], BACK_1, k)
-        sent(yback.at[k, 0:rows - ygroup], BACK_2, k)
-        sent(msend.at[k], MERGE, k)
 
     for k in range(chunks):
         for h in (0, 1) if k >= end else (None,):
@@ -432,11 +455,21 @@
             sent(full_l.at[k, span(h)], SUM_RIGHT2, slot(k, h))
             sent(full_r.at[k, span(h)], SUM_LEFT2, slot(k, h))
 
-    pltpu.make_async_copy(meta.at[0], meta.at[1], send_once.at[META]).wait()
-    pltpu.make_async_copy(tok_ref, tok2.at[0:quarter, tokens:2 * tokens], send_once.at[TOK]).wait()
     pltpu.make_async_copy(afull.at[0:(NX - 1) * part_rank], afull.at[0:(NX - 1) * part_rank],
                           send_once.at[UP_IN]).wait()
     pltpu.make_async_copy(bfull.at[0:NX - 1], bfull.at[0:NX - 1], send_once.at[DOWN_OUT]).wait()
+
+    @pl.loop(max(2, pairs + 2), pairs + 3)
+    def _(t):
+        tick(t)
+
+    for k in range(chunks):
+        width = min(LANES, quarter - k * LANES)
+        out_ref[k * LANES:k * LANES + width, :] = own[k, 0:width, :].astype(BF16)
+
+    @pl.loop(0, chunks)
+    def _(k):
+        sent(yback.at[k, 0:spread_rows - padded], BACK_2, k)
 
 
 def local(tokens, routes, gates, wup, wdn, aup, bup, adn, bdn):
@@ -445,6 +478,7 @@
     part_rank = aup.shape[2]
     chunks = -(-quarter // LANES)
     rows = SLOTS * NY * NZ
+    padded_rows = 2 * NY * (-(-CAP * NZ // 16) * 16)
     inner = -(-hidden // LANES) * LANES + rank
     grid = (chunks, rows, LANES)
     vmem, hbm = pl.BlockSpec(memory_space=pltpu.VMEM), pl.BlockSpec(memory_space=pl.ANY)
@@ -461,21 +495,22 @@
             pltpu.VMEM((rank, hidden), BF16),
             pltpu.VMEM((rank, hidden), BF16),
             pltpu.VMEM((rank, quarter), BF16),
-            pltpu.VMEM((chunks * LANES, 2 * count), BF16),
-            pltpu.VMEM((2, 8, count), I32),
-            pltpu.VMEM((rows, 2 * count), BF16),
-            pltpu.VMEM((rows, 2 * count), BF16),
-            pltpu.VMEM((rows, 4 * count), BF16),
-            pltpu.VMEM((rows, 4 * count), BF16),
+            pltpu.VMEM((chunks * LANES, count), BF16),
+            pltpu.VMEM((padded_rows, count), BF16),
+            pltpu.VMEM((padded_rows, count), BF16),
+            pltpu.VMEM((padded_rows, 2 * count), BF16),
+            pltpu.VMEM((padded_rows, 2 * count), BF16),
             pltpu.VMEM((rows, rows), BF16),
+            pltpu.VMEM((rows, padded_rows), BF16),
+            pltpu.VMEM((padded_rows, rows), BF16),
             pltpu.VMEM((1, hidden, NX * quarter), BF16),
             pltpu.VMEM((1, hidden, NX * quarter), BF16),
             pltpu.VMEM((rank, NX * quarter), BF16),
             pltpu.VMEM((NX, rank, quarter), BF16),
             pltpu.VMEM((chunks, inner, NX * LANES), BF16),
             pltpu.VMEM((chunks, inner, NX * LANES), BF16),
-            pltpu.VMEM(grid, BF16),
-            pltpu.VMEM(grid, BF16),
+            pltpu.VMEM((chunks, padded_rows, LANES), BF16),
+            pltpu.VMEM((chunks, padded_rows, LANES), BF16),
             pltpu.VMEM(grid, BF16),
             pltpu.VMEM(grid, BF16),
             pltpu.VMEM((chunks, NX, rows, LANES), BF16),
@@ -489,15 +524,13 @@
             pltpu.VMEM((rows, LANES), BF16),
             pltpu.VMEM(grid, BF16),
             pltpu.VMEM(grid, BF16),
-            pltpu.VMEM(grid, BF16),
-            pltpu.VMEM(grid, BF16),
-            pltpu.VMEM((chunks, LANES, count), F32),
-            pltpu.VMEM((chunks, LANES, count), F32),
+            pltpu.VMEM((chunks, padded_rows, LANES), BF16),
+            pltpu.VMEM((chunks, padded_rows, LANES), BF16),
             pltpu.VMEM((chunks, LANES, count), F32),
             pltpu.SemaphoreType.DMA((KINDS, 2 * chunks)),
             pltpu.SemaphoreType.DMA((KINDS, 2 * chunks)),
-            pltpu.SemaphoreType.DMA((4,)),
-            pltpu.SemaphoreType.DMA((4,)),
+            pltpu.SemaphoreType.DMA((2,)),
+            pltpu.SemaphoreType.DMA((2,)),
             pltpu.SemaphoreType.DMA((9,)),
         ],
         compiler_params=pltpu.CompilerParams(

time: 120 us -> 118 us (0.983)
  Pallas kernels: 119 us -> 116 us
    pallas_call x1, Pallas kernels: 119 us -> 116 us  [local(): pl.pallas_call(functools.partial(kernel, chunks), out_shape=jax.ShapeDtyp...]
where the time goes in v3:
time: 118 us
  Pallas kernels  116 us (98%)
  local copies, waits for them, and re-layouts  1.61 us (1%)
    pallas_call x1, Pallas kernels, local(): pl.pallas_call(functools.partial(kernel, chunks), out_shape=jax.ShapeDtyp...  116 us

profile of v3, /device:TPU:1, one launch (start us, length us, event | category | flops | bytes accessed | tf_op | source)
XLA Modules:
  0.0 117.8 jit_solution(626387389982599862)
XLA Ops:
  0.0 116.2 %shard_map.91 = bf16[720,128]{1,0:T(8,128)(2,1)} custom-call(s32[4,128]{1,0:T(4,128)} %bitcast.20, s32[4,128]{1,0:T(4,128)} %bitcast.21, bf16[720,128]{1,0:T(8,128)(2,1)} %bitcast.15, bf16[1,360,2880]{2,1,0:T(8,128)(2,1)} %bitcast.14, bf16[1,360,2880]{2,1,0:T(8,128)(2,1)} %wdn_hbm.1, bf16[16,2880]{1,0:T(8,128)(2,1)} %bitcast.17, bf16[64,360]{1,0:T(8,128)(2,1)} %bitcast.18, ...), custom_call_target="tpu_custom_call" | custom-call | flops 8000000000 | bytes 6000000 | tf_op jit(solution)/shard_map/pallas_call | solution.py:485
  116.2 1.6 %copy.11 = bf16[128,720]{0,1:T(8,128)(2,1)} copy(bf16[128,720]{0,1:T(8,128)(2,1)} %bitcast.13) | data formatting | bytes 368640

commit v4 on v3

--- a/solution.py
+++ b/solution.py
@@ -310,11 +310,6 @@
         step(t, pass_on, 0, 1, 1)
         step(t, choose, -2, 0, 0)
         step(t, choose, -2, 1, 1)
-
-        @pl.when(t == 0)
-        def _():
-            weigh()
-            order_split()
 
         step(t, forward, 2, 0)
         step(t, spread, 1, 0, 0)
@@ -413,12 +408,14 @@
         add_half(2)
         if pairs > 2:
             partial(4)
+    order_split()
     add_full(0, 0, 0)
     add_full(0, 0, 1)
     if more:
         add_half(3)
         if pairs > 2:
             partial(5)
+    weigh()
     add_full(1, 1, 0)
     add_full(1, 1, 1)
 

time: 118 us -> 118 us (level)
  no operation moved by 1% of the time
where the time goes in v4:
time: 118 us
  Pallas kernels  116 us (98%)
  local copies, waits for them, and re-layouts  1.61 us (1%)
    pallas_call x1, Pallas kernels, local(): pl.pallas_call(functools.partial(kernel, chunks), out_shape=jax.ShapeDtyp...  116 us

profile of v4, /device:TPU:1, one launch (start us, length us, event | category | flops | bytes accessed | tf_op | source)
XLA Modules:
  0.0 117.8 jit_solution(16311994292402232796)
XLA Ops:
  0.0 116.2 %shard_map.91 = bf16[720,128]{1,0:T(8,128)(2,1)} custom-call(s32[4,128]{1,0:T(4,128)} %bitcast.20, s32[4,128]{1,0:T(4,128)} %bitcast.21, bf16[720,128]{1,0:T(8,128)(2,1)} %bitcast.15, bf16[1,360,2880]{2,1,0:T(8,128)(2,1)} %bitcast.14, bf16[1,360,2880]{2,1,0:T(8,128)(2,1)} %wdn_hbm.1, bf16[16,2880]{1,0:T(8,128)(2,1)} %bitcast.17, bf16[64,360]{1,0:T(8,128)(2,1)} %bitcast.18, ...), custom_call_target="tpu_custom_call" | custom-call | flops 8000000000 | bytes 6000000 | tf_op jit(solution)/shard_map/pallas_call | solution.py:482
  116.2 1.6 %copy.11 = bf16[128,720]{0,1:T(8,128)(2,1)} copy(bf16[128,720]{0,1:T(8,128)(2,1)} %bitcast.13) | data formatting | bytes 368640
